TPU v7x, 32 devices: a whole 2x2x4 slice. The times are simulated.
32 devices in a mesh: groups: 2 (over y), pair: 4 (over x, core), tensor: 4 (over z).
Axes of the slice: x: 2, y: 2, z: 4, core: 2. Of those that a mesh axis runs over, the one named last changes fastest.
Arguments:
- x_clean: bfloat16 [1024, 8192], P('groups', 'pair'), parts along dimension 0, may hold values from -6 to 6
- x_corr: bfloat16 [1024, 8192], P('groups', 'pair'), parts along dimension 0, may hold values from -6 to 6
- cotangent: bfloat16 [1024, 8192], P('groups', 'pair'), parts along dimension 0, may hold values from -6 to 6
- w_gate: bfloat16 [8192, 14336], P('pair', 'tensor'), may hold values from -0.0625 to 0.0625
- w_up: bfloat16 [8192, 14336], P('pair', 'tensor'), may hold values from -0.0625 to 0.0625
- w_down: bfloat16 [14336, 8192], P('tensor', 'pair'), may hold values from -0.0625 to 0.0625
- start: int32 [64], P(('groups', 'pair')), parts along dimension 0, may hold values from 0 to 7
- partners: int32 [64, 3], P(('groups', 'pair')), parts along dimension 0, may hold values from -1 to 31, as said below
Outputs:
- scores: float32 [64, 14336], P(('groups', 'pair'), 'tensor'), parts along dimension 0
- input_grad: bfloat16 [1024, 8192], P('groups', 'pair'), parts along dimension 0
There are 2 independent parts, one for each index of `groups`. A program takes and returns all parts, laid end to end along the dimension named above; an argument that names none is the same for every part. Nothing has to cross between parts.
Inputs may be any that keep to these rules, and one draw needn't show every extreme that they name: Each clean prompt has 1 to 3 partners in its first slots and -1 in the rest; every corrupted prompt is the first partner of exactly one clean prompt; a partner may repeat within a prompt's slots.
All inputs are finite; a program needn't handle non-finite values.
Results may differ from a plain program's by a relative error of at most 0.02.
Values may be sent and summed in bfloat16 or wider, within the bound.
A program may use at most 192 MiB of HBM per device.

v0:
```python
import jax
import jax.numpy as jnp
from jax import lax
from jax.experimental import pallas as pl
from jax.experimental.pallas import tpu as pltpu
from jax.sharding import PartitionSpec as P

SEQ = 16
CHUNKS = 2
VMEM_BYTES = 64 * 2**20 - 2**18


def silu_grad(value):
    sig = jax.nn.sigmoid(value)
    return sig * (1.0 + value * (1.0 - sig))


def make_body(n_pair):
    chips = n_pair // 2
    to_core = [(q, q ^ 1) for q in range(n_pair)]

    def to_chip(shift):
        return [(q, ((q // 2 + shift) % chips) * 2 + q % 2) for q in range(n_pair)]

    def columns(value, at, width):
        return lax.dynamic_slice_in_dim(value, at * width, width, axis=1)

    def body(x_clean, x_corr, cotangent, w_gate, w_up, w_down, start, partners):
        tokens = x_clean.shape[0]
        neurons = w_gate.shape[1]
        half = neurons // 2
        block = half // chips
        index = lax.axis_index("pair")
        core = index % 2
        chip = index // 2
        transposed = (((1,), (1,)), ((), ()))

        def reduce(part):
            arrived = lax.ppermute(columns(part, 1 - core, half), "pair", to_core)
            local = columns(part, core, half).astype(jnp.float32) + arrived.astype(jnp.float32)
            local = local.astype(jnp.bfloat16)
            total = columns(local, chip, block).astype(jnp.float32)
            for shift in range(1, chips):
                piece = columns(local, (chip + shift) % chips, block)
                total = total + lax.ppermute(piece, "pair", to_chip(shift)).astype(jnp.float32)
            return total

        def gather(own):
            rows = own.shape[0]
            mine = jnp.zeros((rows, half), own.dtype)
            mine = lax.dynamic_update_slice_in_dim(mine, own, chip * block, axis=1)
            for shift in range(1, chips):
                piece = lax.ppermute(own, "pair", to_chip(shift))
                source = (chip - shift + chips) % chips
                mine = lax.dynamic_update_slice_in_dim(mine, piece, source * block, axis=1)
            other = lax.ppermute(mine, "pair", to_core)
            first = core == 0
            return jnp.concatenate(
                [jnp.where(first, mine, other), jnp.where(first, other, mine)], axis=1
            )

        def project(left, weight):
            return jnp.dot(left, weight, preferred_element_type=jnp.float32).astype(jnp.bfloat16)

        def project_back(left, weight):
            return lax.dot_general(
                left, weight, transposed, preferred_element_type=jnp.float32
            ).astype(jnp.bfloat16)

        partners_all = lax.all_gather(partners, "pair", axis=0, tiled=True)
        start_all = lax.all_gather(start, "pair", axis=0, tiled=True)

        rows = tokens // CHUNKS
        summed = []
        for k in range(CHUNKS):
            at = slice(k * rows, (k + 1) * rows)
            gate_c = reduce(project(x_clean[at], w_gate))
            up_c = reduce(project(x_clean[at], w_up))
            grad_h = reduce(project_back(cotangent[at], w_down))
            summed.append((gate_c, up_c, grad_h))

        acts, grads, out = [], [], []
        for gate_c, up_c, grad_h in summed:
            silu_c = jax.nn.silu(gate_c)
            acts.append(silu_c * up_c)
            grads.append(grad_h)
            d_gate = gather((grad_h * up_c * silu_grad(gate_c)).astype(jnp.bfloat16))
            d_up = gather((grad_h * silu_c).astype(jnp.bfloat16))
            partial = lax.dot_general(
                d_gate, w_gate, transposed, preferred_element_type=jnp.float32
            )
            partial = partial + lax.dot_general(
                d_up, w_up, transposed, preferred_element_type=jnp.float32
            )
            partial = partial.astype(jnp.bfloat16)
            if out:
                partial, out[-1] = lax.optimization_barrier((partial, out[-1]))
            out.append(lax.psum(partial, "tensor"))
        input_grad = jnp.concatenate(out, axis=0)

        gate_r = reduce(project(x_corr, w_gate))
        up_r = reduce(project(x_corr, w_up))
        act_r = (jax.nn.silu(gate_r) * up_r).astype(jnp.bfloat16)
        act_c = jnp.concatenate(acts, axis=0)
        grad_h = jnp.concatenate(grads, axis=0)

        prompts = tokens // SEQ
        row = jnp.arange(tokens, dtype=jnp.int32)
        used = (partners_all >= 0).astype(jnp.float32)
        mixing = jnp.zeros((tokens, tokens), jnp.float32)
        for slot in range(partners.shape[1]):
            picked = jnp.repeat(partners_all[:, slot], SEQ)
            wanted = jnp.where(picked >= 0, picked * SEQ + row % SEQ, -1)
            mixing = mixing + (wanted[:, None] == row[None, :]).astype(jnp.float32)
        total = jnp.dot(mixing.astype(jnp.bfloat16), act_r, preferred_element_type=jnp.float32)
        count = jnp.repeat(jnp.sum(used, axis=1), SEQ)
        keep = (row % SEQ >= jnp.repeat(start_all, SEQ)).astype(jnp.float32)
        weighted = keep[:, None] * (total - count[:, None] * act_c) * grad_h
        own = jnp.sum(weighted.reshape(prompts, SEQ, block), axis=1) / SEQ
        share = prompts // n_pair
        placed = lax.all_to_all(
            own.reshape(n_pair, share, block), "pair", split_axis=0, concat_axis=0, tiled=True
        )
        placed = placed.reshape(chips, 2, share, block)
        scores = placed.transpose(2, 1, 0, 3).reshape(share, neurons)
        return (scores, input_grad)

    return body


TILE = 256
SLOTS = 2
MESH = pl.DeviceIdType.MESH
F32 = jnp.float32
BF16 = jnp.bfloat16


def fused(
    x_clean, x_corr, cotangent, start, partners, w_gate, w_up, w_down,
    scores, input_grad,
    ring_n, ring_t, ring_b, core_out, core_in, sums, chip_in, grads, part, half_in, quarter_in,
    act_c, grad_h, act_r, mixing, scale, table, own_scores,
    ring_n_sem, ring_t_sem, ring_b_sem, core_out_sem, core_in_sem, chip_out_sem, chip_in_sem,
    dx_out, dx_in, dc_out, dc_in, z_out, z_in, table_out, table_in, score_out, score_in,
):
    tokens, width = x_clean.shape
    rows = tokens // CHUNKS
    neurons = w_gate.shape[1]
    half = neurons // 2
    block = half // 2
    share = partners.shape[0]
    prompts = tokens // SEQ
    index = lax.axis_index("pair")
    depth = lax.axis_index("tensor")
    core = lax.rem(index, 2)
    chip = index // 2
    sibling = chip * 2 + (1 - core)
    across = (1 - chip) * 2 + core
    diagonal = (1 - chip) * 2 + (1 - core)
    others = (sibling, across, diagonal)
    odd = lax.rem(depth, 2)
    high = depth // 2
    z_near = high * 2 + (1 - odd)
    z_far = (1 - high) * 2 + odd
    mine = core * 2 + chip
    transposed = (((1,), (1,)), ((), ()))

    def remote(src, dst, send, recv, **where):
        return pltpu.make_async_remote_copy(
            src_ref=src, dst_ref=dst, send_sem=send, recv_sem=recv,
            device_id=where, device_id_type=MESH,
        )

    barrier = pltpu.get_barrier_semaphore()
    for other in others:
        pl.semaphore_signal(barrier, inc=1, device_id={"pair": other}, device_id_type=MESH)
    for other in (z_near, z_far):
        pl.semaphore_signal(barrier, inc=1, device_id={"tensor": other}, device_id_type=MESH)

    units = []
    for k in range(CHUNKS):
        units += [(x_clean, w_gate, False, k), (x_clean, w_up, False, k), (cotangent, w_down, True, k)]
    for k in range(CHUNKS):
        units += [(x_corr, w_gate, False, k), (x_corr, w_up, False, k)]
    tiles = half // TILE

    def tile_copy(u, side, parity, i):
        _, weight, flipped, _ = units[u]
        at = pl.ds(pl.multiple_of(side * half + i * TILE, TILE), TILE)
        slot = parity * SLOTS + lax.rem(i, SLOTS)
        if flipped:
            return pltpu.make_async_copy(weight.at[at, :], ring_t.at[slot], ring_t_sem.at[slot])
        return pltpu.make_async_copy(weight.at[:, at], ring_n.at[slot], ring_n_sem.at[slot])

    stages = [("out", 0)]
    for u in range(len(units)):
        if u + 1 < len(units):
            stages.append(("out", u + 1))
        stages.append(("own", u))
    flow = {"at": 0}

    def side_of(kind):
        return 1 - core if kind == "out" else core

    def prefetch(s):
        if s < len(stages):
            kind, u = stages[s]
            for i in range(SLOTS):
                tile_copy(u, side_of(kind), s % 2, jnp.int32(i)).start()

    def core_copy(u):
        return remote(
            core_out.at[u % 2], core_in.at[u % 4], core_out_sem.at[u % 2], core_in_sem.at[u % 4],
            pair=sibling,
        )

    def chip_copy(u):
        at = pl.ds(pl.multiple_of((1 - chip) * block, 128), block)
        return remote(
            sums.at[u, :, at], chip_in.at[u], chip_out_sem.at[u], chip_in_sem.at[u], pair=across
        )

    def stage():
        s = flow["at"]
        flow["at"] = s + 1
        kind, u = stages[s]
        left, _, flipped, k = units[u]
        prefetch(s + 1)
        if kind == "out" and u >= 2:
            core_copy(u - 2).wait_send()
        if kind == "own":
            core_copy(u).wait_recv()

        def step(i, carry):
            tile_copy(u, side_of(kind), s % 2, i).wait()
            slot = (s % 2) * SLOTS + lax.rem(i, SLOTS)
            at = pl.ds(pl.multiple_of(i * TILE, TILE), TILE)
            lhs = left[k * rows:(k + 1) * rows, :]
            if flipped:
                value = lax.dot_general(lhs, ring_t[slot], transposed, preferred_element_type=F32)
            else:
                value = jnp.dot(lhs, ring_n[slot], preferred_element_type=F32)
            if kind == "out":
                core_out[u % 2, :, at] = value.astype(BF16)
            else:
                value = value + core_in[u % 4, :, at].astype(F32)
                sums[u, :, at] = value.astype(BF16)

            @pl.when(i + SLOTS < tiles)
            def _():
                tile_copy(u, side_of(kind), s % 2, i + SLOTS).start()

            return carry

        lax.fori_loop(0, tiles, step, 0)
        if kind == "out":
            core_copy(u).start()

    def run_to(u):
        while stages[flow["at"] - 1] != ("own", u) or flow["at"] == 0:
            stage()

    own_at = pl.ds(pl.multiple_of(chip * block, 128), block)

    def total(u, at):
        return sums[u, at, own_at].astype(F32) + chip_in[u, at, :].astype(F32)

    def grad_copy(k, a):
        return remote(
            grads.at[k, a, mine], grads.at[k, a, mine], dx_out.at[2 * k + a], dx_in.at[2 * k + a],
            pair=across,
        )

    def grad_share(k, a):
        at = pl.ds(core * 2, 2)
        return remote(
            grads.at[k, a, at], grads.at[k, a, at], dc_out.at[2 * k + a], dc_in.at[2 * k + a],
            pair=sibling,
        )

    def finish_clean(k):
        for u in range(3 * k, 3 * k + 3):
            chip_copy(u).wait_recv()

        def step(i, carry):
            at = pl.ds(pl.multiple_of(i * 16, 16), 16)
            gate, up, grad = (total(3 * k + j, at) for j in range(3))
            sig = jax.nn.sigmoid(gate)
            silu = gate * sig
            grads[k, 0, mine, at, :] = (grad * up * (sig * (1.0 + gate * (1.0 - sig)))).astype(BF16)
            grads[k, 1, mine, at, :] = (grad * silu).astype(BF16)
            place = pl.ds(pl.multiple_of(k * rows + i * 16, 16), 16)
            act_c[place, :] = silu * up
            grad_h[place, :] = grad
            return carry

        lax.fori_loop(0, rows // 16, step, 0)
        for a in range(2):
            grad_copy(k, a).start()

    def finish_corr(k):
        first = 3 * CHUNKS + 2 * k
        for u in (first, first + 1):
            chip_copy(u).wait_recv()

        def step(i, carry):
            at = pl.ds(pl.multiple_of(i * 16, 16), 16)
            gate, up = total(first, at), total(first + 1, at)
            place = pl.ds(pl.multiple_of(k * rows + i * 16, 16), 16)
            act_r[place, :] = (gate * jax.nn.sigmoid(gate) * up).astype(BF16)
            return carry

        lax.fori_loop(0, rows // 16, step, 0)

    def back_copy(a, i):
        slot = lax.rem(i, SLOTS)
        at = pl.ds(pl.multiple_of(i * TILE, TILE), TILE)
        weight = (w_gate, w_up)[a]
        return pltpu.make_async_copy(
            weight.at[at, :], ring_b.at[a, slot], ring_b_sem.at[a, slot]
        )

    def back(k):
        steps = width // TILE
        for i in range(SLOTS):
            for a in range(2):
                back_copy(a, jnp.int32(i)).start()
        for a in range(2):
            grad_copy(k, a).wait_recv()
            grad_share(k, a).start()
        for a in range(2):
            grad_share(k, a).wait_recv()

        def step(i, carry):
            slot = lax.rem(i, SLOTS)
            value = jnp.zeros((rows, TILE), F32)
            for a in range(2):
                back_copy(a, i).wait()
                for b in range(4):
                    value = value + lax.dot_general(
                        grads[k, a, b], ring_b[a, slot, :, b * block:(b + 1) * block],
                        transposed, preferred_element_type=F32,
                    )
            part[k, :, pl.ds(pl.multiple_of(i * TILE, TILE), TILE)] = value.astype(BF16)

            @pl.when(i + SLOTS < steps)
            def _():
                for a in range(2):
                    back_copy(a, i + SLOTS).start()

            return carry

        lax.fori_loop(0, steps, step, 0)

    half_rows = rows // 2
    quarter_rows = rows // 4

    def z_copy(k, n):
        sems = z_out.at[4 * k + n], z_in.at[4 * k + n]
        if n == 0:
            at = pl.ds(pl.multiple_of((1 - odd) * half_rows, 16), half_rows)
            return remote(part.at[k, at, :], half_in.at[k], *sems, tensor=z_near)
        if n == 1:
            at = pl.ds(
                pl.multiple_of(odd * half_rows + (1 - high) * quarter_rows, 16), quarter_rows
            )
            return remote(part.at[k, at, :], quarter_in.at[k], *sems, tensor=z_far)
        if n == 2:
            at = pl.ds(
                pl.multiple_of(k * rows + odd * half_rows + high * quarter_rows, 16), quarter_rows
            )
            return remote(input_grad.at[at, :], input_grad.at[at, :], *sems, tensor=z_far)
        at = pl.ds(pl.multiple_of(k * rows + odd * half_rows, 16), half_rows)
        return remote(input_grad.at[at, :], input_grad.at[at, :], *sems, tensor=z_near)

    def z_step(k, n):
        z_copy(k, n).wait_recv()
        if n == 0:
            z_copy(k, n).wait_send()

            def step(i, carry):
                at = pl.ds(pl.multiple_of(odd * half_rows + i * 16, 16), 16)
                here = pl.ds(pl.multiple_of(i * 16, 16), 16)
                part[k, at, :] = (
                    part[k, at, :].astype(F32) + half_in[k, here, :].astype(F32)
                ).astype(BF16)
                return carry

            lax.fori_loop(0, half_rows // 16, step, 0)
        if n == 1:

            def step(i, carry):
                local = odd * half_rows + high * quarter_rows + i * 16
                at = pl.ds(pl.multiple_of(local, 16), 16)
                place = pl.ds(pl.multiple_of(k * rows + local, 16), 16)
                here = pl.ds(pl.multiple_of(i * 16, 16), 16)
                input_grad[place, :] = (
                    part[k, at, :].astype(F32) + quarter_in[k, here, :].astype(F32)
                ).astype(BF16)
                return carry

            lax.fori_loop(0, quarter_rows // 16, step, 0)
        if n < 3:
            z_copy(k, n + 1).start()

    def table_copy(n):
        return remote(
            table.at[index], table.at[index], table_out.at[n], table_in.at[n], pair=others[n]
        )

    def score_copy(n):
        at = pl.ds(pl.multiple_of(mine * block, 128), block)
        return remote(
            own_scores.at[others[n]], scores.at[:, at], score_out.at[n], score_in.at[n],
            pair=others[n],
        )

    prefetch(0)
    lane = lax.broadcasted_iota(jnp.int32, (share, 128), 1)
    counts = jnp.zeros((share, 128), F32)
    used = jnp.zeros((share, 1), F32)
    for slot in range(partners.shape[1]):
        picked = partners[:, slot:slot + 1]
        counts = counts + (lane == picked).astype(F32)
        used = used + (picked >= 0).astype(F32)
    counts = jnp.where(lane == 126, start[...].astype(F32), counts)
    table[index] = jnp.where(lane == 127, used, counts)
    pl.semaphore_wait(barrier, 5)
    for n in range(3):
        table_copy(n).start()

    last_clean = 3 * CHUNKS - 1
    for u in range(last_clean + 1):
        run_to(u)
        chip_copy(u).start()

    for n in range(3):
        table_copy(n).wait_recv()
    spread = (
        lax.broadcasted_iota(jnp.int32, (tokens, prompts), 0) // SEQ
        == lax.broadcasted_iota(jnp.int32, (tokens, prompts), 1)
    ).astype(BF16)
    by_row = jnp.dot(
        spread, table[...].reshape(prompts, 128).astype(BF16), preferred_element_type=F32
    )
    position = lax.rem(lax.broadcasted_iota(jnp.int32, (tokens, 1), 0), SEQ)
    keep = (position.astype(F32) >= by_row[:, 126:127]).astype(F32)
    scale[...] = jnp.broadcast_to(keep * by_row[:, 127:128], (tokens, 128))
    widen = (
        lax.broadcasted_iota(jnp.int32, (128, tokens), 1) // SEQ
        == lax.broadcasted_iota(jnp.int32, (128, tokens), 0)
    ).astype(BF16)
    wide = jnp.dot((keep * by_row).astype(BF16), widen, preferred_element_type=F32)
    same = position == lax.rem(lax.broadcasted_iota(jnp.int32, (tokens, tokens), 1), SEQ)
    mixing[...] = jnp.where(same, wide, 0.0).astype(BF16)

    finish_clean(0)
    first_corr = 3 * CHUNKS
    run_to(first_corr + 1)
    finish_clean(1)
    run_to(first_corr + 3)
    back(0)
    z_copy(0, 0).start()
    chip_copy(first_corr).start()
    chip_copy(first_corr + 1).start()
    back(1)
    z_copy(1, 0).start()
    chip_copy(first_corr + 2).start()
    chip_copy(first_corr + 3).start()
    z_step(0, 0)
    z_step(0, 1)
    z_step(1, 0)
    z_step(0, 2)
    z_step(1, 1)
    finish_corr(0)
    z_step(1, 2)
    finish_corr(1)

    span = share * SEQ

    def score_step(i, carry):
        at = pl.ds(pl.multiple_of(i * span, span), span)
        mixed = jnp.dot(mixing[at, :], act_r[...], preferred_element_type=F32)
        value = (mixed - scale[at, 0:1] * act_c[at, :]) * grad_h[at, :]
        own_scores[i] = jnp.sum(value.reshape(share, SEQ, block), axis=1) * (1.0 / SEQ)
        return carry

    lax.fori_loop(0, prompts // share, score_step, 0)
    for n in range(3):
        score_copy(n).start()
    scores[:, pl.ds(pl.multiple_of(mine * block, 128), block)] = own_scores[index]

    z_copy(0, 3).wait_recv()
    z_copy(1, 3).wait_recv()
    for n in range(3):
        score_copy(n).wait()
        table_copy(n).wait_send()
    for u in (len(units) - 2, len(units) - 1):
        core_copy(u).wait_send()
    for u in range(len(units)):
        chip_copy(u).wait_send()
    for k in range(CHUNKS):
        for a in range(2):
            grad_copy(k, a).wait_send()
            grad_share(k, a).wait_send()
        for n in range(1, 4):
            z_copy(k, n).wait_send()


def fused_body(x_clean, x_corr, cotangent, w_gate, w_up, w_down, start, partners):
    tokens, width = x_clean.shape
    neurons = w_gate.shape[1]
    rows, half = tokens // CHUNKS, neurons // 2
    block = half // 2
    share = start.shape[0]
    prompts = tokens // SEQ
    units = 5 * CHUNKS
    vmem = pl.BlockSpec(memory_space=pltpu.VMEM)
    anywhere = pl.BlockSpec(memory_space=pl.ANY)
    dma = pltpu.SemaphoreType.DMA
    scores, input_grad = pl.pallas_call(
        fused,
        out_shape=(
            jax.ShapeDtypeStruct((share, neurons), F32),
            jax.ShapeDtypeStruct((tokens, width), BF16),
        ),
        in_specs=[vmem] * 5 + [anywhere] * 3,
        out_specs=(vmem, vmem),
        scratch_shapes=[
            pltpu.VMEM((2 * SLOTS, width, TILE), BF16),
            pltpu.VMEM((2 * SLOTS, TILE, width), BF16),
            pltpu.VMEM((2, SLOTS, TILE, neurons), BF16),
            pltpu.VMEM((2, rows, half), BF16),
            pltpu.VMEM((4, rows, half), BF16),
            pltpu.VMEM((units, rows, half), BF16),
            pltpu.VMEM((units, rows, block), BF16),
            pltpu.VMEM((CHUNKS, 2, 4, rows, block), BF16),
            pltpu.VMEM((CHUNKS, rows, width), BF16),
            pltpu.VMEM((CHUNKS, rows // 2, width), BF16),
            pltpu.VMEM((CHUNKS, rows // 4, width), BF16),
            pltpu.VMEM((tokens, block), F32),
            pltpu.VMEM((tokens, block), F32),
            pltpu.VMEM((tokens, block), BF16),
            pltpu.VMEM((tokens, tokens), BF16),
            pltpu.VMEM((tokens, 128), F32),
            pltpu.VMEM((prompts // share, share, 128), F32),
            pltpu.VMEM((prompts // share, share, block), F32),
            dma((2 * SLOTS,)), dma((2 * SLOTS,)), dma((2, SLOTS)),
            dma((2,)), dma((4,)), dma((units,)), dma((units,)),
            dma((2 * CHUNKS,)), dma((2 * CHUNKS,)), dma((2 * CHUNKS,)), dma((2 * CHUNKS,)),
            dma((4 * CHUNKS,)), dma((4 * CHUNKS,)),
            dma((3,)), dma((3,)), dma((3,)), dma((3,)),
        ],
        compiler_params=pltpu.CompilerParams(
            collective_id=0, has_side_effects=True, vmem_limit_bytes=VMEM_BYTES
        ),
        name="attribution",
    )(x_clean, x_corr, cotangent, start.reshape(share, 1), partners, w_gate, w_up, w_down)
    return scores, input_grad


def fits(mesh, x_clean, w_gate):
    if mesh.shape["pair"] != 4 or mesh.shape["tensor"] != 4:
        return False
    neurons = w_gate.shape[1] // mesh.shape["tensor"]
    tokens = x_clean.shape[0] // mesh.shape["groups"]
    width = x_clean.shape[1] // mesh.shape["pair"]
    small = tokens <= 512 and width <= 2048 and neurons <= 3584
    return small and neurons % (2 * TILE) == 0 and (neurons // 4) % 128 == 0


def solution(mesh):
    placed = (
        P("groups", "pair"),
        P("groups", "pair"),
        P("groups", "pair"),
        P("pair", "tensor"),
        P("pair", "tensor"),
        P("tensor", "pair"),
        P(("groups", "pair")),
        P(("groups", "pair"), None),
    )

    def run(*args):
        body = fused_body if fits(mesh, args[0], args[3]) else make_body(mesh.shape["pair"])
        return jax.shard_map(
            body,
            mesh=mesh,
            in_specs=placed,
            out_specs=(P(("groups", "pair"), "tensor"), P("groups", "pair")),
            check_vma=False,
        )(*args)

    return run
```

profile of v0, /device:TPU:0, one launch (start us, length us, event | category | flops | bytes accessed | tf_op | source)
XLA Modules:
  0.0 239.7 jit_solution(11681162040347623295)
XLA Ops:
  0.6 1.3 copy.10.start
  2.0 1.3 copy.11.partners
  3.3 231.7 %attribution.1 = (f32[8,3584]{1,0:T(8,128)}, bf16[512,2048]{1,0:T(8,128)(2,1)}) custom-call(bf16[512,2048]{1,0:T(8,128)(2,1)} %x_clean.1, bf16[512,2048]{1,0:T(8,128)(2,1)} %x_corr.1, bf16[512,2048]{1,0:T(8,128)(2,1)} %cotangent.1, s32[8,1]{1,0:T(8,128)} %copy.10.start, s32[8,3]{1,0:T(8,128)} %copy.11.partners, bf16[2048,3584]{1,0:T(8,128)(2,1)} %w_gate.1, ...), custom_call_target="tpu_custom_call" | custom-call | tf_op jit(solution)/shard_map/attribution/pallas_call | solution.py:521
  235.0 1.6 copy.14
  236.6 3.2 %copy.15 = bf16[512,2048]{1,0:T(8,128)(2,1)} copy(bf16[512,2048]{1,0:T(8,128)(2,1)} %get-tuple-element.5) | data formatting | bytes 4194304
where the time goes:
time: 241 us; the launch traced here: 240 us
  Pallas kernels  232 us (96%)
  local copies, waits for them, and re-layouts  7.38 us (3%)
    pallas_call x1, Pallas kernels, fused_body(): pl.pallas_call(fused, out_shape=(jax.ShapeDtypeStruct((share, neurons), F...  232 us
    unnamed x3, local copies, waits for them, and re-layouts  6.06 us

commit v1 on v0

--- a/solution.py
+++ b/solution.py
@@ -7,6 +7,7 @@
 
 SEQ = 16
 CHUNKS = 2
+STREAMS = 4
 VMEM_BYTES = 64 * 2**20 - 2**18
 
 
@@ -136,18 +137,23 @@
 
 
 def fused(
-    x_clean, x_corr, cotangent, start, partners, w_gate, w_up, w_down,
+    x_clean, start, partners, x_corr, cotangent, w_gate, w_up, w_down,
     scores, input_grad,
     ring_n, ring_t, ring_b, core_out, core_in, sums, chip_in, grads, part, half_in, quarter_in,
     act_c, grad_h, act_r, mixing, scale, table, own_scores,
     ring_n_sem, ring_t_sem, ring_b_sem, core_out_sem, core_in_sem, chip_out_sem, chip_in_sem,
     dx_out, dx_in, dc_out, dc_in, z_out, z_in, table_out, table_in, score_out, score_in,
+    cotangent_in, x_corr_in, late_sem,
 ):
     tokens, width = x_clean.shape
     rows = tokens // CHUNKS
     neurons = w_gate.shape[1]
     half = neurons // 2
     block = half // 2
+    late = {
+        2: pltpu.make_async_copy(cotangent, cotangent_in, late_sem.at[0]),
+        3 * CHUNKS: pltpu.make_async_copy(x_corr, x_corr_in, late_sem.at[1]),
+    }
     share = partners.shape[0]
     prompts = tokens // SEQ
     index = lax.axis_index("pair")
@@ -179,9 +185,9 @@
 
     units = []
     for k in range(CHUNKS):
-        units += [(x_clean, w_gate, False, k), (x_clean, w_up, False, k), (cotangent, w_down, True, k)]
+        units += [(x_clean, w_gate, False, k), (x_clean, w_up, False, k), (cotangent_in, w_down, True, k)]
     for k in range(CHUNKS):
-        units += [(x_corr, w_gate, False, k), (x_corr, w_up, False, k)]
+        units += [(x_corr_in, w_gate, False, k), (x_corr_in, w_up, False, k)]
     tiles = half // TILE
 
     def tile_copy(u, side, parity, i):
@@ -228,6 +234,8 @@
         prefetch(s + 1)
         if kind == "out" and u >= 2:
             core_copy(u - 2).wait_send()
+        if kind == "out" and u in late:
+            late[u].wait()
         if kind == "own":
             core_copy(u).wait_recv()
 
@@ -257,7 +265,7 @@
             core_copy(u).start()
 
     def run_to(u):
-        while stages[flow["at"] - 1] != ("own", u) or flow["at"] == 0:
+        while ("own", u) not in stages[: flow["at"]]:
             stage()
 
     own_at = pl.ds(pl.multiple_of(chip * block, 128), block)
@@ -350,39 +358,45 @@
 
             return carry
 
-        lax.fori_loop(0, steps, step, 0)
+        for h in range(STREAMS):
+            lax.fori_loop(h * steps // STREAMS, (h + 1) * steps // STREAMS, step, 0)
+            z_copy(k, 0, h).start()
 
     half_rows = rows // 2
     quarter_rows = rows // 4
 
-    def z_copy(k, n):
-        sems = z_out.at[4 * k + n], z_in.at[4 * k + n]
+    stream = width // STREAMS
+
+    def z_copy(k, n, h):
+        which = (k * STREAMS + h) * 4 + n
+        sems = z_out.at[which], z_in.at[which]
+        cols = pl.ds(h * stream, stream)
         if n == 0:
             at = pl.ds(pl.multiple_of((1 - odd) * half_rows, 16), half_rows)
-            return remote(part.at[k, at, :], half_in.at[k], *sems, tensor=z_near)
+            return remote(part.at[k, at, cols], half_in.at[k, :, cols], *sems, tensor=z_near)
         if n == 1:
             at = pl.ds(
                 pl.multiple_of(odd * half_rows + (1 - high) * quarter_rows, 16), quarter_rows
             )
-            return remote(part.at[k, at, :], quarter_in.at[k], *sems, tensor=z_far)
+            return remote(part.at[k, at, cols], quarter_in.at[k, :, cols], *sems, tensor=z_far)
         if n == 2:
             at = pl.ds(
                 pl.multiple_of(k * rows + odd * half_rows + high * quarter_rows, 16), quarter_rows
             )
-            return remote(input_grad.at[at, :], input_grad.at[at, :], *sems, tensor=z_far)
+            return remote(input_grad.at[at, cols], input_grad.at[at, cols], *sems, tensor=z_far)
         at = pl.ds(pl.multiple_of(k * rows + odd * half_rows, 16), half_rows)
-        return remote(input_grad.at[at, :], input_grad.at[at, :], *sems, tensor=z_near)
-
-    def z_step(k, n):
-        z_copy(k, n).wait_recv()
+        return remote(input_grad.at[at, cols], input_grad.at[at, cols], *sems, tensor=z_near)
+
+    def z_step(k, n, h):
+        z_copy(k, n, h).wait_recv()
+        cols = pl.ds(h * stream, stream)
         if n == 0:
-            z_copy(k, n).wait_send()
 
             def step(i, carry):
                 at = pl.ds(pl.multiple_of(odd * half_rows + i * 16, 16), 16)
                 here = pl.ds(pl.multiple_of(i * 16, 16), 16)
-                part[k, at, :] = (
-                    part[k, at, :].astype(F32) + half_in[k, here, :].astype(F32)
+                part[k, at, cols] = (
+                    part[k, at, cols].astype(F32) + half_in[k, here, cols].astype(F32)
                 ).astype(BF16)
                 return carry
 
@@ -394,14 +408,14 @@
                 at = pl.ds(pl.multiple_of(local, 16), 16)
                 place = pl.ds(pl.multiple_of(k * rows + local, 16), 16)
                 here = pl.ds(pl.multiple_of(i * 16, 16), 16)
-                input_grad[place, :] = (
-                    part[k, at, :].astype(F32) + quarter_in[k, here, :].astype(F32)
+                input_grad[place, cols] = (
+                    part[k, at, cols].astype(F32) + quarter_in[k, here, cols].astype(F32)
                 ).astype(BF16)
                 return carry
 
             lax.fori_loop(0, quarter_rows // 16, step, 0)
         if n < 3:
-            z_copy(k, n + 1).start()
+            z_copy(k, n + 1, h).start()
 
     def table_copy(n):
         return remote(
@@ -416,6 +430,8 @@
         )
 
     prefetch(0)
+    for copy in late.values():
+        copy.start()
     lane = lax.broadcasted_iota(jnp.int32, (share, 128), 1)
     counts = jnp.zeros((share, 128), F32)
     used = jnp.zeros((share, 1), F32)
@@ -429,10 +445,19 @@
     for n in range(3):
         table_copy(n).start()
 
-    last_clean = 3 * CHUNKS - 1
-    for u in range(last_clean + 1):
-        run_to(u)
-        chip_copy(u).start()
+    def send(*which):
+        for u in which:
+            run_to(u)
+            chip_copy(u).start()
+
+    def z_all(k, n):
+        for h in range(STREAMS):
+            z_step(k, n, h)
+
+    first_corr = 3 * CHUNKS
+    send(0, 1, 2, 3)
+    finish_clean(0)
+    send(4, 5)
 
     for n in range(3):
         table_copy(n).wait_recv()
@@ -454,26 +479,20 @@
     same = position == lax.rem(lax.broadcasted_iota(jnp.int32, (tokens, tokens), 1), SEQ)
     mixing[...] = jnp.where(same, wide, 0.0).astype(BF16)
 
-    finish_clean(0)
-    first_corr = 3 * CHUNKS
+    back(0)
+    run_to(first_corr)
+    z_all(0, 0)
     run_to(first_corr + 1)
+    z_all(0, 1)
     finish_clean(1)
-    run_to(first_corr + 3)
-    back(0)
-    z_copy(0, 0).start()
-    chip_copy(first_corr).start()
-    chip_copy(first_corr + 1).start()
+    send(first_corr, first_corr + 1, first_corr + 2)
+    z_all(0, 2)
+    send(first_corr + 3)
     back(1)
-    z_copy(1, 0).start()
-    chip_copy(first_corr + 2).start()
-    chip_copy(first_corr + 3).start()
-    z_step(0, 0)
-    z_step(0, 1)
-    z_step(1, 0)
-    z_step(0, 2)
-    z_step(1, 1)
+    z_all(1, 0)
     finish_corr(0)
-    z_step(1, 2)
+    z_all(1, 1)
+    z_all(1, 2)
     finish_corr(1)
 
     span = share * SEQ
@@ -490,8 +509,9 @@
         score_copy(n).start()
     scores[:, pl.ds(pl.multiple_of(mine * block, 128), block)] = own_scores[index]
 
-    z_copy(0, 3).wait_recv()
-    z_copy(1, 3).wait_recv()
+    for k in range(CHUNKS):
+        for h in range(STREAMS):
+            z_copy(k, 3, h).wait_recv()
     for n in range(3):
         score_copy(n).wait()
         table_copy(n).wait_send()
@@ -503,8 +523,9 @@
         for a in range(2):
             grad_copy(k, a).wait_send()
             grad_share(k, a).wait_send()
-        for n in range(1, 4):
-            z_copy(k, n).wait_send()
+        for n in range(4):
+            for h in range(STREAMS):
+                z_copy(k, n, h).wait_send()
 
 
 def fused_body(x_clean, x_corr, cotangent, w_gate, w_up, w_down, start, partners):
@@ -524,7 +545,7 @@
             jax.ShapeDtypeStruct((share, neurons), F32),
             jax.ShapeDtypeStruct((tokens, width), BF16),
         ),
-        in_specs=[vmem] * 5 + [anywhere] * 3,
+        in_specs=[vmem] * 3 + [anywhere] * 5,
         out_specs=(vmem, vmem),
         scratch_shapes=[
             pltpu.VMEM((2 * SLOTS, width, TILE), BF16),
@@ -548,14 +569,15 @@
             dma((2 * SLOTS,)), dma((2 * SLOTS,)), dma((2, SLOTS)),
             dma((2,)), dma((4,)), dma((units,)), dma((units,)),
             dma((2 * CHUNKS,)), dma((2 * CHUNKS,)), dma((2 * CHUNKS,)), dma((2 * CHUNKS,)),
-            dma((4 * CHUNKS,)), dma((4 * CHUNKS,)),
+            dma((4 * CHUNKS * STREAMS,)), dma((4 * CHUNKS * STREAMS,)),
             dma((3,)), dma((3,)), dma((3,)), dma((3,)),
+            pltpu.VMEM((tokens, width), BF16), pltpu.VMEM((tokens, width), BF16), dma((2,)),
         ],
         compiler_params=pltpu.CompilerParams(
             collective_id=0, has_side_effects=True, vmem_limit_bytes=VMEM_BYTES
         ),
         name="attribution",
-    )(x_clean, x_corr, cotangent, start.reshape(share, 1), partners, w_gate, w_up, w_down)
+    )(x_clean, start.reshape(share, 1), partners, x_corr, cotangent, w_gate, w_up, w_down)
     return scores, input_grad
 
 

time: 241 us -> 221 us (0.917)
  Pallas kernels: 232 us -> 212 us
    pallas_call x1, Pallas kernels: 232 us -> 212 us  [fused_body(): pl.pallas_call(fused, out_shape=(jax.ShapeDtypeStruct((share, neurons), F...]
where the time goes in v1:
time: 221 us; the launch traced here: 220 us
  Pallas kernels  212 us (96%)
  local copies, waits for them, and re-layouts  7.38 us (3%)
    pallas_call x1, Pallas kernels, fused_body(): pl.pallas_call(fused, out_shape=(jax.ShapeDtypeStruct((share, neurons), F...  212 us
    unnamed x3, local copies, waits for them, and re-layouts  6.06 us

profile of v1, /device:TPU:0, one launch (start us, length us, event | category | flops | bytes accessed | tf_op | source)
XLA Modules:
  0.0 219.6 jit_solution(5923254428435547992)
XLA Ops:
  0.6 1.3 copy.10.start
  2.0 1.3 copy.11.partners
  3.3 211.6 %attribution.1 = (f32[8,3584]{1,0:T(8,128)}, bf16[512,2048]{1,0:T(8,128)(2,1)}) custom-call(bf16[512,2048]{1,0:T(8,128)(2,1)} %x_clean.1, s32[8,1]{1,0:T(8,128)} %copy.10.start, s32[8,3]{1,0:T(8,128)} %copy.11.partners, bf16[512,2048]{1,0:T(8,128)(2,1)} %x_corr.1, bf16[512,2048]{1,0:T(8,128)(2,1)} %cotangent.1, bf16[2048,3584]{1,0:T(8,128)(2,1)} %w_gate.1, ...), custom_call_target="tpu_custom_call" | custom-call | tf_op jit(solution)/shard_map/attribution/pallas_call | solution.py:542
  214.9 1.6 copy.14
  216.5 3.2 %copy.15 = bf16[512,2048]{1,0:T(8,128)(2,1)} copy(bf16[512,2048]{1,0:T(8,128)(2,1)} %get-tuple-element.5) | data formatting | bytes 4194304
